TPU v7x, 128 devices: a whole 4x4x4 slice. The times are simulated.
128 devices in a mesh: grp: 4 (over z), had: 32 (over x, y, core).
Axes of the slice: x: 4, y: 4, z: 4, core: 2. Of those that a mesh axis runs over, the one named last changes fastest.
Arguments:
- embeddings: bfloat16 [131072, 1024], P(('grp', 'had'))
- targets: bfloat16 [131072, 64], P(('grp', 'had'))
- sign_bits: int32 [131072], P(('grp', 'had')), may hold values 0 or 1
- samples: int32 [128, 32, 16], P(('grp', 'had')), may hold values from 0 to 1023, as said below
- counts: int32 [128, 32], P(('grp', 'had')), may hold values from 1 to 16, as said below
Outputs:
- basis_rows: float32 [65536, 1024], P(('grp', 'had'))
- coefficients: float32 [1024, 64], replicated
Inputs may be any that keep to these rules, and one draw needn't show every extreme that they name: `samples`: entry c of list [o, s] is a row number within source device s of owner o's group; the first counts[o, s] entries of a list are distinct, the rest are padding. `counts`: in every draw each owner takes 16 rows from some source device, and some owner takes 16 rows from every source device.
All inputs are finite; a program needn't handle non-finite values. No bound on the sum of `sign_bits` on one device may be relied on, other than what follows from the above.
Results may differ from a plain program's by a relative error of at most 0.0003.
Values sent between devices are 32-bit elements; how exact they have to be, the bound alone decides.
No kernel may reach another device: no remote copies, remote signals or barrier semaphores. Data moves between devices by JAX's collectives and lax.ppermute only.
A program may use at most 128 MiB of HBM per device.

v0:
```python
import math

import jax
import jax.numpy as jnp
from jax import lax
from jax.sharding import PartitionSpec as P

D = 1024


def partner_2(value, axis, stride):
    mask = 2**stride
    pairs = [(source, source ^ mask) for source in range(lax.axis_size(axis))]
    return lax.ppermute(value, axis, pairs)


def hadamard_table(size):
    row_ids = jnp.arange(size, dtype=jnp.int32)[:, None]
    col_ids = jnp.arange(size, dtype=jnp.int32)[None, :]
    correlation = jnp.bitwise_and(row_ids, col_ids)
    parity = jnp.zeros((size, size), jnp.int32)
    for bit_pos in range(max(size.bit_length(), 1)):
        parity = jnp.bitwise_xor(parity, jnp.bitwise_and(jnp.right_shift(correlation, bit_pos), 1))
    return (1 - 2 * parity).astype(jnp.float32)


def route_samples(mixed_rows, samples, had_size, slot_count, columns):
    own_lists = samples.reshape(had_size, slot_count)
    requested = lax.all_to_all(own_lists, "had", split_axis=0, concat_axis=0, tiled=True)
    outgoing = jnp.take(mixed_rows, requested.reshape(-1), axis=0).reshape(
        had_size, slot_count, columns
    )
    return lax.all_to_all(outgoing, "had", split_axis=0, concat_axis=0, tiled=True)


def on_device(embeddings, targets, sign_bits, samples, counts):
    row_count = embeddings.shape[0]
    had_size = lax.axis_size("had")
    slot_count = samples.shape[2]
    factor = (1 - 2 * sign_bits).astype(jnp.bfloat16)[:, None]
    joined = jnp.concatenate([embeddings, targets], axis=1) * factor
    columns = joined.shape[1]
    inner_mix = jnp.dot(
        hadamard_table(row_count).astype(jnp.bfloat16), joined, preferred_element_type=jnp.float32
    )
    norm_factor = 1.0 / math.sqrt(row_count * had_size)
    current = inner_mix
    position = lax.axis_index("had")
    for bit_pos in range(had_size.bit_length() - 1):
        partner = partner_2(current, "had", bit_pos)
        upper_half = jnp.bitwise_and(jnp.right_shift(position, bit_pos), 1) == 1
        current = jnp.where(upper_half, partner - current, current + partner)
    mixed_rows = current * norm_factor
    received = route_samples(mixed_rows, samples, had_size, slot_count, columns)
    live_slots = (
        jnp.arange(slot_count, dtype=jnp.int32)[None, :] < counts.reshape(had_size)[:, None]
    )
    sketch = jnp.where(live_slots[..., None], received, jnp.zeros_like(received)).reshape(
        had_size * slot_count, columns
    )
    gram_part = lax.dot_general(
        sketch,
        sketch[:, :D],
        (((0,), (0,)), ((), ())),
        precision=lax.Precision.HIGHEST,
        preferred_element_type=jnp.float32,
    )
    gram_total = lax.psum(gram_part, ("grp", "had"))
    slot_total = lax.axis_size("grp") * had_size * had_size * slot_count
    gram_total = gram_total * (1.0 / slot_total)
    system = gram_total[:D] + 0.05 * jnp.eye(D, dtype=jnp.float32)
    factor_lower = jnp.linalg.cholesky(system)
    basis_rows = lax.linalg.triangular_solve(
        factor_lower, sketch[:, :D], left_side=False, lower=True, transpose_a=True
    )
    right_side = gram_total[D:].T
    middle = lax.linalg.triangular_solve(factor_lower, right_side, left_side=True, lower=True)
    coefficients = lax.linalg.triangular_solve(
        factor_lower, middle, left_side=True, lower=True, transpose_a=True
    )
    return (basis_rows, coefficients)


def solution(mesh):
    placed = (
        P(("grp", "had"), None),
        P(("grp", "had"), None),
        P(("grp", "had")),
        P(("grp", "had"), None, None),
        P(("grp", "had"), None),
    )
    return jax.shard_map(
        on_device,
        mesh=mesh,
        in_specs=placed,
        out_specs=(P(("grp", "had"), None), P()),
        check_vma=False,
    )
```

profile of v0, /device:TPU:1, one launch (start us, length us, event | category | flops | bytes accessed | tf_op | source)
XLA Modules:
  0.0 1068.6 jit_solution(10728327982703286921)
XLA Ops:
  8.9 11.1 %fusion.1 = f32[1024,1088]{0,1:T(8,128)} fusion(bf16[1024,64]{1,0:T(8,128)(2,1)S(1)} %copy.53, bf16[1024,1024]{1,0:T(8,128)(2,1)} %param.5, bf16[1024]{0:T(1024)(128)(2,1)S(1)} %subtract_convert_fusion), kind=kOutput, calls=%fused_computation.16 | convolution fusion | flops 2327183360 | bytes 6686720 | tf_op jit(solution)/shard_map/dot_general | solution.py:43
  37.6 96.3 %collective-permute-done.1 = f32[1024,1088]{0,1:T(8,128)} collective-permute-done((f32[1024,1088]{0,1:T(8,128)}, f32[1024,1088]{0,1:T(8,128)}, u32[]{:S(2)}, u32[]{:S(2)}) %collective-permute-start.1) | collective-permute-done | bytes 4456480 | tf_op jit(solution)/shard_map/ppermute | solution.py:14
  144.2 95.4 %collective-permute-done.2 = f32[1024,1088]{0,1:T(8,128)} collective-permute-done((f32[1024,1088]{0,1:T(8,128)}, f32[1024,1088]{0,1:T(8,128)}, u32[]{:S(2)}, u32[]{:S(2)}) %collective-permute-start.2) | collective-permute-done | bytes 4456480 | tf_op jit(solution)/shard_map/ppermute | solution.py:14
  248.6 94.6 %collective-permute-done.3 = f32[1024,1088]{0,1:T(8,128)} collective-permute-done((f32[1024,1088]{0,1:T(8,128)}, f32[1024,1088]{0,1:T(8,128)}, u32[]{:S(2)}, u32[]{:S(2)}) %collective-permute-start.3) | collective-permute-done | bytes 4456480 | tf_op jit(solution)/shard_map/ppermute | solution.py:14
  362.5 90.6 %all-to-all-done = s32[32,1,16]{2,1,0:T(1,128)S(1)} async-done(((s32[32,1,16]{2,1,0:T(1,128)}), s32[32,1,16]{2,1,0:T(1,128)S(1)}, u32[]{:S(2)}, u32[]{:S(2)}) %all-to-all-start) | async-done | bytes 2080 | tf_op jit(solution)/shard_map/all_to_all | solution.py:29
  480.5 31.1 %all-to-all-done.1 = f32[32,16,1088]{2,1,0:T(8,128)} async-done(((f32[32,16,1088]{2,1,0:T(8,128)}), f32[32,16,1088]{2,1,0:T(8,128)}, u32[]{:S(2)}, u32[]{:S(2)}) %all-to-all-start.1) | async-done | bytes 2228256 | tf_op jit(solution)/shard_map/all_to_all | solution.py:33
  513.4 10.3 fusion.4
  523.7 153.9 %all-reduce.3.cloned.1.call-done = f32[1088,1024]{0,1:T(8,128)} async-done(((f32[1088,1024]{0,1:T(8,128)}), f32[1088,1024]{0,1:T(8,128)}) %all-reduce.3.cloned.1.call-update) | async-done | bytes 4456464 | tf_op jit(solution)/shard_map/psum | solution.py:68
  697.0 11.7 %cholesky.222 = f32[128,128]{1,0:T(8,128)S(1)} custom-call(f32[128,128]{1,0:T(8,128)S(1)} %cholesky.577), custom_call_target="Cholesky" | custom-call | tf_op jit(solution)/shard_map/jit(cholesky)/cholesky | solution.py:72
  708.9 9.8 custom-call.66
  724.4 11.7 %cholesky.243 = f32[128,128]{1,0:T(8,128)S(1)} custom-call(f32[128,128]{1,0:T(8,128)S(1)} %cholesky.581), custom_call_target="Cholesky" | custom-call | tf_op jit(solution)/shard_map/jit(cholesky)/cholesky | solution.py:72
  737.1 10.6 custom-call.67
  753.7 11.7 %cholesky.466 = f32[128,128]{1,0:T(8,128)S(1)} custom-call(f32[128,128]{1,0:T(8,128)S(1)} %cholesky.586), custom_call_target="Cholesky" | custom-call | tf_op jit(solution)/shard_map/jit(cholesky)/cholesky | solution.py:72
  766.2 9.8 custom-call.68
  780.8 11.7 %cholesky.485 = f32[128,128]{1,0:T(8,128)S(1)} custom-call(f32[128,128]{1,0:T(8,128)S(1)} %cholesky.591), custom_call_target="Cholesky" | custom-call | tf_op jit(solution)/shard_map/jit(cholesky)/cholesky | solution.py:72
  793.3 9.8 custom-call.69
  807.4 11.9 %cholesky.504 = f32[128,128]{1,0:T(8,128)S(1)} custom-call(f32[128,128]{1,0:T(8,128)S(1)} %cholesky.596), custom_call_target="Cholesky" | custom-call | tf_op jit(solution)/shard_map/jit(cholesky)/cholesky | solution.py:72
  820.0 9.8 custom-call.70
  834.0 11.7 %cholesky.524 = f32[128,128]{1,0:T(8,128)S(1)} custom-call(f32[128,128]{1,0:T(8,128)S(1)} %cholesky.601), custom_call_target="Cholesky" | custom-call | tf_op jit(solution)/shard_map/jit(cholesky)/cholesky | solution.py:72
  846.5 9.8 custom-call.71
  860.4 11.7 %cholesky.544 = f32[128,128]{1,0:T(8,128)S(1)} custom-call(f32[128,128]{1,0:T(8,128)S(1)} %cholesky.606), custom_call_target="Cholesky" | custom-call | tf_op jit(solution)/shard_map/jit(cholesky)/cholesky | solution.py:72
  885.7 11.7 %cholesky.562 = f32[128,128]{1,0:T(8,128)S(1)} custom-call(f32[128,128]{1,0:T(8,128)S(1)} %convolution_subtract_fusion.17), custom_call_target="Cholesky" | custom-call | tf_op jit(solution)/shard_map/jit(cholesky)/cholesky | solution.py:72
  912.7 28.7 %while.1 = (s32[]{:T(128)}, f32[1024,1024]{0,1:T(8,128)}, s32[8,2]{0,1:T(2,128)S(1)}, f32[8,128,128]{2,1,0:T(8,128)}, s32[]{:T(128)}) while((s32[]{:T(128)}, f32[1024,1024]{0,1:T(8,128)}, s32[8,2]{0,1:T(2,128)S(1)}, f32[8,128,128]{2,1,0:T(8,128)}, s32[]{:T(128)}) %tuple.80), condition=%wide.while_cond, body=%wide.while_body.sunk | while | flops 2 | bytes 393329 | solution.py:73
  941.4 79.6 %custom-call.73 = f32[8,128,128]{1,2,0:T(8,128)S(1)} custom-call(f32[8,128,128]{2,1,0:T(8,128)} %get-tuple-element.9), custom_call_target="InvertDiagBlocksLowerTriangular" | custom-call | tf_op jit(solution)/shard_map/triangular_solve | solution.py:73
  (220 shorter events, 232.1 us)
Async XLA Ops:
  20.0 8.9 collective-permute-start
  36.2 97.7 %collective-permute-start.1 = (f32[1024,1088]{0,1:T(8,128)}, f32[1024,1088]{0,1:T(8,128)}, u32[]{:S(2)}, u32[]{:S(2)}) collective-permute-start(f32[1024,1088]{0,1:T(8,128)} %add_select_fusion.3), channel_id=1, source_target_pairs={{0,2},{1,3},{2,0},{3,1},{4,6},{5,7},{6,4},{7,5},{8,10},{9,11},{10,... | collective-permute-start | bytes 13369352 | tf_op jit(solution)/shard_map/ppermute | solution.py:14
  141.2 98.3 %collective-permute-start.2 = (f32[1024,1088]{0,1:T(8,128)}, f32[1024,1088]{0,1:T(8,128)}, u32[]{:S(2)}, u32[]{:S(2)}) collective-permute-start(f32[1024,1088]{0,1:T(8,128)} %add_select_fusion.2), channel_id=1, source_target_pairs={{0,4},{1,5},{2,6},{3,7},{4,0},{5,1},{6,2},{7,3},{8,12},{9,13},{10,... | collective-permute-start | bytes 13369352 | tf_op jit(solution)/shard_map/ppermute | solution.py:14
  246.9 96.3 %collective-permute-start.3 = (f32[1024,1088]{0,1:T(8,128)}, f32[1024,1088]{0,1:T(8,128)}, u32[]{:S(2)}, u32[]{:S(2)}) collective-permute-start(f32[1024,1088]{0,1:T(8,128)} %add_select_fusion.1), channel_id=1, source_target_pairs={{0,8},{1,9},{2,10},{3,11},{4,12},{5,13},{6,14},{7,15},{8,0},{9,1},... | collective-permute-start | bytes 13369352 | tf_op jit(solution)/shard_map/ppermute | solution.py:14
  248.6 104.7 %copy-start.6 = (s32[1,32,16]{1,2,0:T(8,128)S(1)}, s32[1,32,16]{1,2,0:T(8,128)}, u32[]{:S(2)}) copy-start(s32[1,32,16]{1,2,0:T(8,128)} %param.8) | copy-start | bytes 6148
  350.5 103.9 %collective-permute-start.4 = (f32[1024,1088]{0,1:T(8,128)}, f32[1024,1088]{0,1:T(8,128)}, u32[]{:S(2)}, u32[]{:S(2)}) collective-permute-start(f32[1024,1088]{0,1:T(8,128)} %add_select_fusion), channel_id=1, source_target_pairs={{0,16},{1,17},{2,18},{3,19},{4,20},{5,21},{6,22},{7,23},{8,24},{9,... | collective-permute-start | bytes 13369352 | tf_op jit(solution)/shard_map/ppermute | solution.py:14
  353.9 99.1 %all-to-all-start = ((s32[32,1,16]{2,1,0:T(1,128)}), s32[32,1,16]{2,1,0:T(1,128)S(1)}, u32[]{:S(2)}, u32[]{:S(2)}) async-start(s32[32,1,16]{2,1,0:T(1,128)} %bitcast.1), calls=%async_computation | async-start | bytes 32768 | tf_op jit(solution)/shard_map/all_to_all | solution.py:29
  473.0 7.5 copy-start.8
  474.6 37.0 %all-to-all-start.1 = ((f32[32,16,1088]{2,1,0:T(8,128)}), f32[32,16,1088]{2,1,0:T(8,128)}, u32[]{:S(2)}, u32[]{:S(2)}) async-start(f32[32,16,1088]{2,1,0:T(8,128)} %broadcast_select_fusion.1), calls=%async_computation.1 | async-start | bytes 4718592 | tf_op jit(solution)/shard_map/all_to_all | solution.py:33
  480.4 197.3 %all-reduce.3.cloned.1.call-start = ((), (), s32[]{:S(2)}) async-start(), calls=%async_computation.2 | async-start | bytes 9437184 | tf_op jit(solution)/shard_map/psum | solution.py:68
  680.3 2.1 copy-start.1
  695.1 1.9 copy-start.3
  723.5 24.7 %copy-start.4 = (f32[896,128]{0,1:T(8,128)S(1)}, f32[896,128]{0,1:T(8,128)}, u32[]{:S(2)}) copy-start(f32[896,128]{0,1:T(8,128)} %copy.58) | copy-start | bytes 1376260
  747.7 1.0 copy-start.5
  749.3 2.0 copy-start
  1021.0 8.0 copy-start.2
  1037.4 6.8 copy-start.7
Sparse Core Ops, SparseCore 0:
  523.8 153.7 all-reduce.2
where the time goes:
time: 1080 us; the launch traced here: 1070 us
  waiting for transfers between devices  569 us (53%)
  other arithmetic  304 us (28%)
  matrix products  85.5 us (8%)
  local copies, waits for them, and re-layouts  64.5 us (6%)
  starting transfers between devices  24.6 us (2%)
  between operations  20.1 us (2%)
    ppermute x5, waiting for transfers between devices, partner_2(): return lax.ppermute(value, axis, pairs)  294 us
    another operation x30, other arithmetic, on_device(): factor_lower = jnp.linalg.cholesky(system)  169 us
    psum x1, waiting for transfers between devices, on_device(): gram_total = lax.psum(gram_part, ('grp', 'had'))  154 us
    all_to_all x1, waiting for transfers between devices, route_samples(): lax.all_to_all(own_lists, 'had', split_axis=0, concat_axis=0, tiled=True)  90.6 us
    another operation x3, other arithmetic, on_device(): lax.linalg.triangular_solve(factor_lower, sketch[:, :D], left_side=False,...  84.4 us
    all_to_all x1, waiting for transfers between devices, route_samples(): lax.all_to_all(outgoing, 'had', split_axis=0, concat_axis=0, tiled=True)  31.1 us
    select_n x4, other arithmetic, on_device(): current = jnp.where(upper_half, partner - current, current + partner)  29.2 us
    another operation x40, local copies, waits for them, and re-layouts  28.6 us
  transfers between devices with their start and end apart: 8, of which 7 were waited for; matrix products, arithmetic and copies ran while one was open for 0% of the time, Pallas kernels for 0%

commit v1 on v0

v1 whole, which is shorter than its diff:
```python
import math

import jax
import jax.numpy as jnp
from jax import lax
from jax.experimental import pallas as pl
from jax.experimental.pallas import tpu as pltpu
from jax.sharding import PartitionSpec as P

D = 1024
K = 64
CAP = 16
HAD = 32
ROWS = 1024
SLOTS = 512
LANES = 128
BLOCK = 128
BLOCKS = D // BLOCK
RIDGE = 0.05
BOTH = ("grp", "had")

PIECE = 280
LIST_ROW = 272
BACK = 136
HIGHEST = lax.Precision.HIGHEST
COLUMN_ROWS = [D + K - BLOCK * j for j in range(BLOCKS)]
COLUMN_START = [sum(COLUMN_ROWS[:j]) for j in range(BLOCKS)]
PACKED = sum(COLUMN_ROWS)
MIB = 1024 * 1024


def call(kernel, out_shape, scratch, vmem_mib, *args):
    return pl.pallas_call(
        kernel,
        out_shape=out_shape,
        in_specs=[pl.BlockSpec(memory_space=pltpu.VMEM)] * len(args),
        out_specs=jax.tree.map(lambda _: pl.BlockSpec(memory_space=pltpu.VMEM), out_shape),
        scratch_shapes=scratch,
        compiler_params=pltpu.CompilerParams(vmem_limit_bytes=vmem_mib * MIB),
    )(*args)


def f32(*shape):
    return jax.ShapeDtypeStruct(shape, jnp.float32)


def spread_kernel(embeddings, targets, factor, lists, out):
    for tile in range(8):
        rows = slice(tile * LANES, (tile + 1) * LANES)
        sign = factor[tile : tile + 1, :]
        columns = embeddings[rows, :].astype(jnp.float32).T * sign
        out[:, tile * 32 : (tile + 1) * 32, :] = columns.reshape(HAD, 32, LANES)
        extra = targets[rows, :].astype(jnp.float32).T * sign
        for device in range(HAD):
            for half in range(2):
                row = 256 + 2 * tile + half
                source = 32 * half + device
                out[device, row : row + 1, :] = extra[source : source + 1, :]
    tail = jnp.concatenate([lists[...], jnp.zeros((4, LANES), jnp.float32)], axis=0)
    out[:, LIST_ROW:PIECE, :] = jnp.broadcast_to(tail[None], (HAD, 8, LANES))


def swap_segments(values):
    values = list(values)
    lane = lax.broadcasted_iota(jnp.int32, values[0].shape, values[0].ndim - 1)
    for bit in range(3):
        step = 1 << bit
        upper = jnp.bitwise_and(jnp.right_shift(lane, 4 + bit), 1) == 1
        for low in range(8):
            if low & step:
                continue
            first, second = values[low], values[low + step]
            values[low] = jnp.where(upper, pltpu.roll(second, 16 * step, 1), first)
            values[low + step] = jnp.where(upper, second, pltpu.roll(first, LANES - 16 * step, 1))
    return values


def signs(row_bits, count):
    both = jnp.bitwise_and(lax.broadcasted_iota(jnp.int32, (count, row_bits.shape[1]), 0), row_bits)
    for shift in (4, 2, 1):
        both = jnp.bitwise_xor(both, jnp.right_shift(both, shift))
    return (1 - 2 * jnp.bitwise_and(both, 1)).astype(jnp.float32)


def mix_kernel(pieces, out, mixed, lists, table, picked, extra):
    scale = 1.0 / math.sqrt(ROWS * HAD)

    def butterfly(chunk, _):
        rows = pl.ds(pl.multiple_of(chunk * 8, 8), 8)
        values = [pieces[device, rows, :] for device in range(HAD)]
        for bit in range(5):
            step = 1 << bit
            for low in range(HAD):
                if low & step:
                    continue
                first, second = values[low], values[low + step]
                values[low], values[low + step] = first + second, first - second
        for source in range(HAD):
            mixed[source, rows, :] = values[source]
        return 0

    lax.fori_loop(0, LIST_ROW // 8, butterfly, 0)
    for high in range(4):
        received = [pieces[high * 8 + low, LIST_ROW:PIECE, :] for low in range(8)]
        for low, value in enumerate(swap_segments(received)):
            lists[low, :, high * LANES : (high + 1) * LANES] = value

    def source_group(group, _):
        for low in range(8):
            source = group * 8 + low
            rows = lists[low, pl.ds(group, 1), :].astype(jnp.int32)
            fine = signs(jnp.bitwise_and(rows, 31), 32).astype(jnp.bfloat16)
            coarse = signs(jnp.right_shift(rows, 5), 32).astype(jnp.bfloat16)
            for step in range(32):
                table[low % 2, step * 32 : (step + 1) * 32, :] = fine * coarse[step : step + 1, :]
            main = jnp.concatenate([mixed[source, t * 32 : (t + 1) * 32, :] for t in range(8)], axis=1)
            tail = mixed[source, 256:272, :]
            tail = jnp.concatenate([tail[2 * t : 2 * t + 2, :] for t in range(8)], axis=1)
            main_high = main.astype(jnp.bfloat16).astype(jnp.float32)
            tail_high = tail.astype(jnp.bfloat16).astype(jnp.float32)
            left = jnp.concatenate(
                [
                    main_high,
                    main - main_high,
                    tail_high,
                    tail - tail_high,
                    jnp.zeros((4, ROWS), jnp.float32),
                ],
                axis=0,
            ).astype(jnp.bfloat16)
            product = jnp.dot(left, table[low % 2], preferred_element_type=jnp.float32)
            picked[low, 0:32, :] = (product[0:32] + product[32:64]) * scale
            picked[low, 32:34, :] = (product[64:66] + product[66:68]) * scale
        for high in range(4):
            lanes = slice(high * LANES, (high + 1) * LANES)
            moved = swap_segments([picked[low, :, lanes] for low in range(8)])
            for low, value in enumerate(moved):
                out[high * 8 + low, pl.ds(pl.multiple_of(group * 32, 32), 32), :] = value[0:32]
                extra[group, high * 8 + low] = value[32:40]
        return 0

    lax.fori_loop(0, 4, source_group, 0)
    for group in range(4):
        for owner in range(HAD):
            out[owner, 128 + 2 * group : 130 + 2 * group, :] = extra[group, owner, 0:2, :]


def gram_kernel(received, live, gram, sketch, flipped):
    for group in range(4):
        lanes = slice(group * LANES, (group + 1) * LANES)
        keep = live[group : group + 1, :] > 0
        part = received[:, group * 32 : (group + 1) * 32, :].reshape(D, LANES)
        part = jnp.where(keep, part, 0.0)
        flipped[0:D, lanes] = part
        sketch[lanes, :] = part.T
        for half in range(2):
            for device in range(HAD):
                row = D + 32 * half + device
                source = 128 + 2 * group + half
                value = received[device, source : source + 1, :]
                flipped[row : row + 1, lanes] = jnp.where(keep, value, 0.0)
    for pair in range(BLOCKS // 2):
        first = 256 * pair
        block = jnp.dot(
            flipped[first:, :],
            sketch[:, first : first + 256],
            precision=HIGHEST,
            preferred_element_type=jnp.float32,
        )
        left, right = 2 * pair, 2 * pair + 1
        gram[COLUMN_START[left] : COLUMN_START[left] + COLUMN_ROWS[left], :] = block[:, :BLOCK]
        gram[COLUMN_START[right] : COLUMN_START[right] + COLUMN_ROWS[right], :] = block[BLOCK:, BLOCK:]


def across_lanes(value, lane):
    return jnp.broadcast_to(value[:, lane : lane + 1], value.shape)


def down_rows(value, row):
    return jnp.broadcast_to(value[row : row + 1, :], value.shape)


def inverse_factor(block):
    rows = [block[8 * g : 8 * g + 8, :] for g in range(16)]
    sub = lax.broadcasted_iota(jnp.int32, (8, LANES), 0)
    lane = lax.broadcasted_iota(jnp.int32, (8, LANES), 1)
    result = []
    for g in range(16):
        own = jnp.right_shift(lane, 3) == g
        columns = [across_lanes(rows[g], 8 * g + k) for k in range(8)]
        value = jnp.where(own, jnp.where(lane == 8 * g + sub, 1.0, 0.0), rows[g])
        finished = jnp.zeros((8, LANES), jnp.float32)
        for i in range(8):
            pivot = down_rows(columns[i], i)
            inverse = 1.0 / pivot
            root = lax.rsqrt(pivot)
            root = root * (1.5 - 0.5 * pivot * root * root)
            here = sub == i
            row = down_rows(value, i)
            finished = jnp.where(here, row * root, finished)
            weight = columns[i] * inverse
            value = jnp.where(here, row * inverse, value - weight * row)
            for k in range(i + 1, 8):
                entry = down_rows(columns[k], i)
                columns[k] = jnp.where(here, entry * inverse, columns[k] - weight * entry)
        result.append(jnp.where(lane <= 8 * g + sub, finished, 0.0))
        solved = [down_rows(value, k) for k in range(8)]
        for h in range(g + 1, 16):
            terms = [across_lanes(rows[h], 8 * g + k) * solved[k] for k in range(8)]
            while len(terms) > 1:
                terms = [terms[t] + terms[t + 1] for t in range(0, len(terms), 2)]
            rows[h] = jnp.where(own, 0.0, rows[h]) - terms[0]
    return jnp.concatenate(result, axis=0)


def times_transposed(left, right):
    return lax.dot_general(
        left,
        right,
        (((1,), (1,)), ((), ())),
        precision=HIGHEST,
        preferred_element_type=jnp.float32,
    )


def times(left, right):
    return jnp.dot(left, right, precision=HIGHEST, preferred_element_type=jnp.float32)


def solve_kernel(slot_total, gram, sketch, basis, coefficients, lower, inverses):
    row = lax.broadcasted_iota(jnp.int32, (BLOCK, BLOCK), 0)
    column = lax.broadcasted_iota(jnp.int32, (BLOCK, BLOCK), 1)
    ridge = jnp.where(row == column, RIDGE, 0.0)
    for j in range(BLOCKS):
        start = COLUMN_START[j]
        lower[start : start + BLOCK, :] = gram[start : start + BLOCK, :] * (1.0 / slot_total) + ridge
        rest = slice(start + BLOCK, start + COLUMN_ROWS[j])
        lower[rest, :] = gram[rest, :] * (1.0 / slot_total)
    basis[...] = sketch[...]
    for j in range(BLOCKS):
        start = COLUMN_START[j]
        own = slice(BLOCK * j, BLOCK * (j + 1))
        inverse = inverse_factor(lower[start : start + BLOCK, :])
        inverses[j] = inverse
        below = times_transposed(lower[start + BLOCK : start + COLUMN_ROWS[j], :], inverse)
        lower[start + BLOCK : start + COLUMN_ROWS[j], :] = below
        for i in range(j + 1, BLOCKS):
            first = BLOCK * (i - j - 1)
            target = slice(COLUMN_START[i], COLUMN_START[i] + COLUMN_ROWS[i])
            lower[target, :] -= times_transposed(below[first:], below[first : first + BLOCK])
        solved = times_transposed(basis[:, own], inverse)
        basis[:, own] = solved
        if j < BLOCKS - 1:
            rest = slice(BLOCK * (j + 1), D)
            basis[:, rest] -= times_transposed(solved, below[: BLOCK * (BLOCKS - 1 - j)])
    middle = []
    for j in range(BLOCKS):
        end = COLUMN_START[j] + COLUMN_ROWS[j]
        middle.append(lower[end - K : end, :])
    for j in reversed(range(BLOCKS)):
        value = times(middle[j], inverses[j])
        coefficients[BLOCK * j : BLOCK * (j + 1), :] = value.T
        for i in range(j):
            start = COLUMN_START[i] + BLOCK * (j - i)
            middle[i] = middle[i] - times(value, lower[start : start + BLOCK, :])


def total(gram):
    return lax.psum(gram, BOTH)


def on_device(embeddings, targets, sign_bits, samples, counts):
    had_size = lax.axis_size("had")
    factor = (1 - 2 * sign_bits).astype(jnp.float32).reshape(8, LANES)
    lists = samples.reshape(4, LANES).astype(jnp.float32)
    pieces = call(spread_kernel, f32(HAD, PIECE, LANES), [], 40, embeddings, targets, factor, lists)
    pieces = lax.all_to_all(pieces, "had", split_axis=0, concat_axis=0, tiled=True)
    outgoing = call(
        mix_kernel,
        f32(HAD, BACK, LANES),
        [
            pltpu.VMEM((HAD, LIST_ROW, LANES), jnp.float32),
            pltpu.VMEM((8, 8, SLOTS), jnp.float32),
            pltpu.VMEM((2, ROWS, SLOTS), jnp.bfloat16),
            pltpu.VMEM((8, 40, SLOTS), jnp.float32),
            pltpu.VMEM((4, HAD, 8, LANES), jnp.float32),
        ],
        40,
        pieces,
    )
    received = lax.all_to_all(outgoing, "had", split_axis=0, concat_axis=0, tiled=True)
    slot = jnp.arange(CAP, dtype=jnp.int32)[None, :]
    live = (slot < counts.reshape(had_size)[:, None]).astype(jnp.float32).reshape(4, LANES)
    gram, sketch = call(
        gram_kernel,
        (f32(PACKED, LANES), f32(SLOTS, D)),
        [pltpu.VMEM((D + K, SLOTS), jnp.float32)],
        40,
        received,
        live,
    )
    gram = total(gram)
    slot_total = lax.axis_size("grp") * had_size * SLOTS
    return call(
        lambda *refs: solve_kernel(slot_total, *refs),
        (f32(SLOTS, D), f32(D, K)),
        [
            pltpu.VMEM((PACKED, LANES), jnp.float32),
            pltpu.VMEM((BLOCKS, BLOCK, BLOCK), jnp.float32),
        ],
        40,
        gram,
        sketch,
    )


def solution(mesh):
    placed = (
        P(("grp", "had"), None),
        P(("grp", "had"), None),
        P(("grp", "had")),
        P(("grp", "had"), None, None),
        P(("grp", "had"), None),
    )
    return jax.shard_map(
        on_device,
        mesh=mesh,
        in_specs=placed,
        out_specs=(P(("grp", "had"), None), P()),
        check_vma=False,
    )
```

time: 1080 us -> 342 us (0.32)
  waiting for transfers between devices: 569 us -> 178 us
  other arithmetic: 304 us -> 2.07 us
  matrix products: 85.5 us -> 0 us
  Pallas kernels: 0 us -> 65.6 us
  blocking collectives: 0 us -> 63.6 us
  local copies, waits for them, and re-layouts: 64.5 us -> 10.5 us
  starting transfers between devices: 24.6 us -> 4.19 us
    ppermute x5 -> x0, waiting for transfers between devices: 294 us -> none  [partner_2(): return lax.ppermute(value, axis, pairs)]
    another operation x33 -> x0, other arithmetic: 253 us -> none  [the longest x30 169 us: on_device(): factor_lower = jnp.linalg.cholesky(system)]
    all_to_all x2 -> x1, waiting for transfers between devices: 122 us -> 27.7 us  [on_device(): lax.all_to_all(outgoing, 'had', split_axis=0, concat_axis=0, tiled=True)]
    pallas_call x0 -> x4, Pallas kernels: none -> 65.6 us  [call(): pl.pallas_call(kernel, out_shape=out_shape, in_specs=[pl.BlockSpec(memory...]
    another operation x59 -> x0, matrix products: 64.2 us -> none  [the longest x14 27.1 us: on_device(): factor_lower = jnp.linalg.cholesky(system)]
    all_to_all x0 -> x1, blocking collectives: none -> 63.6 us  [on_device(): lax.all_to_all(pieces, 'had', split_axis=0, concat_axis=0, tiled=True)]
    another operation x70 -> x0, local copies, waits for them, and re-layouts: 35.9 us -> none
    select_n x7 -> x0, other arithmetic: 32.7 us -> none  [the longest x4 29.2 us: on_device(): current = jnp.where(upper_half, partner - current, current + partner)]
  transfers between devices with their start and end apart: 8 -> 2, of which waited for: 7 -> 2; matrix products, arithmetic and copies ran while one was open for 0% -> 0% of each run, Pallas kernels for 0% -> 0%
where the time goes in v1:
time: 342 us; the launch traced here: 338 us
  waiting for transfers between devices  178 us (52%)
  Pallas kernels  65.6 us (19%)
  blocking collectives  63.6 us (19%)
  between operations  14.3 us (4%)
  local copies, waits for them, and re-layouts  10.5 us (3%)
  starting transfers between devices  4.19 us (1%)
    psum x1, waiting for transfers between devices, total(): return lax.psum(gram, BOTH)  150 us
    pallas_call x4, Pallas kernels, call(): pl.pallas_call(kernel, out_shape=out_shape, in_specs=[pl.BlockSpec(memory...  65.6 us
    all_to_all x1, blocking collectives, on_device(): lax.all_to_all(pieces, 'had', split_axis=0, concat_axis=0, tiled=True)  63.6 us
    all_to_all x1, waiting for transfers between devices, on_device(): lax.all_to_all(outgoing, 'had', split_axis=0, concat_axis=0, tiled=True)  27.7 us
    unnamed x16, local copies, waits for them, and re-layouts  9.1 us
  transfers between devices with their start and end apart: 2, of which 2 were waited for; matrix products, arithmetic and copies ran while one was open for 0% of the time, Pallas kernels for 0%

profile of v1, /device:TPU:1, one launch (start us, length us, event | category | flops | bytes accessed | tf_op | source)
XLA Modules:
  0.0 338.4 jit_solution(7781155206212683138)
XLA Ops:
  7.2 1.1 copy.11.targets
  8.2 0.7 convert_element_type.13
  9.0 0.1 convert_element_type.14.lists
  9.1 0.7 convert_bitcast_fusion.factor
  9.8 1.6 copy-done.3
  11.4 0.7 shard_map.68
  12.1 63.6 %all_to_all.10.pieces = f32[32,280,128]{2,1,0:T(8,128)S(1)} all-to-all(f32[32,280,128]{2,1,0:T(8,128)S(1)} %shard_map.68), channel_id=1, replica_groups=mesh['grp'=4,'had'=32] {'had'}, dimensions={0} | all-to-all | bytes 9175040 | tf_op jit(solution)/shard_map/all_to_all | solution.py:277
  75.7 9.0 %shard_map.69 = f32[32,136,128]{2,1,0:T(8,128)S(1)} custom-call(f32[32,280,128]{2,1,0:T(8,128)S(1)} %all_to_all.10.pieces), custom_call_target="tpu_custom_call" | custom-call | tf_op jit(solution)/shard_map/pallas_call | solution.py:33
  84.7 1.4 copy-done
  86.1 4.0 %all-to-all-start.1 = ((f32[32,136,128]{2,1,0:T(8,128)}), f32[32,136,128]{2,1,0:T(8,128)S(1)}, u32[]{:S(2)}, u32[]{:S(2)}) async-start(f32[32,136,128]{2,1,0:T(8,128)} %copy-done), calls=%async_computation.1 | async-start | bytes 4456448 | tf_op jit(solution)/shard_map/all_to_all | solution.py:291
  90.0 0.2 all-reduce.2.cloned.1.call-start
  90.3 0.5 broadcast.6
  90.8 0.7 reduce.3
  91.4 0.1 lt.25
  91.6 0.1 lt.27
  91.7 0.1 lt.23
  91.8 27.7 %all-to-all-done.1.received = f32[32,136,128]{2,1,0:T(8,128)S(1)} async-done(((f32[32,136,128]{2,1,0:T(8,128)}), f32[32,136,128]{2,1,0:T(8,128)S(1)}, u32[]{:S(2)}, u32[]{:S(2)}) %all-to-all-start.1) | async-done | bytes 2228256 | tf_op jit(solution)/shard_map/all_to_all | solution.py:291
  119.5 5.2 %shard_map.70 = (f32[5120,128]{1,0:T(8,128)S(1)}, f32[512,1024]{1,0:T(8,128)S(1)}) custom-call(f32[32,136,128]{2,1,0:T(8,128)S(1)} %all-to-all-done.1.received, f32[4,128]{1,0:T(4,128)S(1)} %compare_convert_fusion.live), custom_call_target="tpu_custom_call" | custom-call | tf_op jit(solution)/shard_map/pallas_call | solution.py:33
  124.7 1.5 copy-done.2
  126.2 1.3 copy-done.4
  127.6 150.4 %all-reduce.2.cloned.1.call-done.refs_0_ = f32[5120,128]{1,0:T(8,128)} async-done(((f32[5120,128]{1,0:T(8,128)}), f32[5120,128]{1,0:T(8,128)}) %all-reduce.2.cloned.1.call-update) | async-done | bytes 2621456 | tf_op jit(solution)/shard_map/psum | solution.py:269
  277.9 1.7 copy-done.1
  279.7 50.8 %shard_map.71 = (f32[512,1024]{1,0:T(8,128)}, f32[1024,64]{1,0:T(8,128)S(1)}) custom-call(f32[5120,128]{1,0:T(8,128)S(1)} %copy-done.1, f32[512,1024]{1,0:T(8,128)S(1)} %copy-done.5), custom_call_target="tpu_custom_call" | custom-call | tf_op jit(solution)/shard_map/pallas_call | solution.py:33
  330.4 0.9 copy.12
  (14 shorter events, 0.2 us)
Async XLA Ops:
  9.8 1.6 copy-start.3
  84.7 1.4 copy-start
  86.1 4.7 %copy-start.6 = (s32[1,32]{1,0:T(1,128)S(1)}, s32[1,32]{1,0:T(1,128)}, u32[]{:S(2)}) copy-start(s32[1,32]{1,0:T(1,128)} %param.9) | copy-start | bytes 388
  86.1 33.5 %all-to-all-start.1 = ((f32[32,136,128]{2,1,0:T(8,128)}), f32[32,136,128]{2,1,0:T(8,128)S(1)}, u32[]{:S(2)}, u32[]{:S(2)}) async-start(f32[32,136,128]{2,1,0:T(8,128)} %copy-done), calls=%async_computation.1 | async-start | bytes 4456448 | tf_op jit(solution)/shard_map/all_to_all | solution.py:291
  90.0 187.9 %all-reduce.2.cloned.1.call-start = ((), (), s32[]{:S(2)}) async-start(), calls=%async_computation.2 | async-start | bytes 5242880 | tf_op jit(solution)/shard_map/psum | solution.py:269
  124.7 1.5 copy-start.2
  126.2 1.3 copy-start.4
  127.5 150.4 %copy-start.5 = (f32[512,1024]{1,0:T(8,128)S(1)}, f32[512,1024]{1,0:T(8,128)}, u32[]{:S(2)}) copy-start(f32[512,1024]{1,0:T(8,128)} %copy-done.4) | copy-start | bytes 6291460
  277.9 1.7 copy-start.1
Sparse Core Ops, SparseCore 0:
  127.7 150.2 all-reduce.1
